TPU v7x, 256 devices: a whole 4x4x8 slice. The times are simulated.
256 devices in a mesh: prow: 16 (over z, core), pcol: 16 (over x, y).
Axes of the slice: x: 4, y: 4, z: 8, core: 2. Of those that a mesh axis runs over, the one named last changes fastest.
Arguments:
- rhs: bfloat16 [4, 16, 1024, 128], P(None, 'prow', 'pcol'), may hold values from -6 to 6
- diag_inv: bfloat16 [4, 16, 1024, 1024], P(None, 'prow', 'pcol'), as said below
- panel: bfloat16 [3, 16, 28672, 1024], P(None, 'prow', 'pcol'), may hold values from -0.03125 to 0.03125
- owner: int32 [3, 16, 224, 1], P(None, 'prow', 'pcol'), may hold values from 0 to 15; in each aligned block of 14 rows (0 to 13, 14 to 27, ..., all dimensions but the last counted through in order) at most 2 rows name the same one
- target_block: int32 [3, 16, 224], P(None, 'prow', 'pcol'), may hold values from 0 to 7
- row_map: int32 [3, 16, 224, 128], P(None, 'prow', 'pcol'), may hold values from -1 to 127, as said below
Outputs:
- solution: bfloat16 [4, 16, 1024, 128], P(None, 'prow', 'pcol')
Inputs may be any that keep to these rules, and one draw needn't show every extreme that they name: In each level, the 14 consecutive blocks of one supernode that one index of pcol holds name one owner at most 2 times. `row_map`: -1 marks a padded row. `diag_inv`: zero above the diagonal.
All inputs are finite; a program needn't handle non-finite values.
Results may differ from a plain program's by a relative error of at most 0.02.
Values may be sent and summed in bfloat16 or wider, within the bound.
A program may use at most 64 MiB of HBM per device.

v0:
```python
import jax
import jax.numpy as jnp
from jax import lax
from jax.sharding import PartitionSpec as P

CAP = 2


def placements(owners_here, owners, capacity):
    hits = (owners_here[:, None] == jnp.arange(owners, dtype=jnp.int32)[None, :]).astype(jnp.int32)
    ranks = jnp.sum((jnp.cumsum(hits, axis=0) - 1) * hits, axis=1)
    return owners_here * capacity + ranks


def pack_blocks(update_blocks, position, blocks_here, maps_here, owners, capacity):
    slots = owners * capacity
    edge = update_blocks.shape[1]
    chosen = position[None, :] == jnp.arange(slots, dtype=jnp.int32)[:, None]
    filled = jnp.any(chosen, axis=1)
    values = jnp.einsum(
        "kb,bir->kir",
        chosen.astype(jnp.bfloat16),
        update_blocks,
        preferred_element_type=jnp.float32,
    ).astype(jnp.bfloat16)
    block_sent = jnp.where(filled, jnp.sum(jnp.where(chosen, blocks_here[None, :], 0), axis=1), -1)
    map_sent = jnp.where(
        filled[:, None],
        jnp.sum(jnp.where(chosen[:, :, None], maps_here[None, :, :], 0), axis=1),
        -1,
    )
    return (
        values.reshape(owners, capacity * edge, update_blocks.shape[2]),
        block_sent.reshape(owners, capacity),
        map_sent.reshape(owners, capacity * edge),
    )


def unpack_blocks(values, block_got, map_got, width, edge):
    slots = block_got.shape[0] * block_got.shape[1]
    values = values.reshape(slots, edge, values.shape[2])
    block_got = block_got.reshape(slots)
    map_got = map_got.reshape(slots, edge)
    placed = (map_got[:, :, None] == jnp.arange(edge, dtype=jnp.int32)[None, None, :]).astype(
        jnp.bfloat16
    )
    permuted = jnp.einsum("kid,kir->kdr", placed, values, preferred_element_type=jnp.float32)
    which = (block_got[:, None] == jnp.arange(width // edge, dtype=jnp.int32)[None, :]).astype(
        jnp.float32
    )
    summed = jnp.einsum("kb,kdr->bdr", which, permuted, precision=lax.Precision.HIGHEST)
    return summed.reshape(width, values.shape[2])


def shards(rhs, diag_inv, panel, owner, target_block, row_map):
    levels = rhs.shape[0]
    rows_here = rhs.shape[2]
    nright = rhs.shape[3]
    width = diag_inv.shape[3]
    blocks_dev = owner.shape[2]
    edge = row_map.shape[3]
    owners = lax.axis_size("prow")
    capacity = CAP
    solved = []
    records = []
    carried = None
    for level in range(levels):
        if level == 0:
            rights = rhs[0, 0]
        else:
            carried_here = lax.psum_scatter(carried, "pcol", scatter_dimension=0, tiled=True)
            rights = (rhs[level, 0].astype(jnp.float32) - carried_here).astype(jnp.bfloat16)
        inverse = diag_inv[level, 0]

        def solve_piece(total, piece, start, inverse=inverse):
            return jnp.dot(inverse, piece, preferred_element_type=jnp.float32)

        start_total = jnp.zeros((rows_here, nright), jnp.float32)
        solved_here = solve_piece(
            start_total, lax.all_gather(rights, "pcol", axis=0, tiled=True), jnp.int32(0)
        ).astype(jnp.bfloat16)
        solved.append(solved_here)
        if level < levels - 1:
            factor = panel[level, 0]

            def update_piece(total, piece, start, factor=factor):
                return jnp.dot(factor, piece, preferred_element_type=jnp.float32)

            update_total = jnp.zeros((blocks_dev * edge, nright), jnp.float32)
            update = update_piece(
                update_total, lax.all_gather(solved_here, "pcol", axis=0, tiled=True), jnp.int32(0)
            ).astype(jnp.bfloat16)
            owners_here = owner[level, 0, :, 0]
            position = placements(owners_here, owners, capacity)
            values, block_sent, map_sent = pack_blocks(
                update.reshape(blocks_dev, edge, nright),
                position,
                target_block[level, 0],
                row_map[level, 0],
                owners,
                capacity,
            )
            values_got, block_got, map_got = (
                lax.all_to_all(values, "prow", split_axis=0, concat_axis=0, tiled=True),
                lax.all_to_all(block_sent, "prow", split_axis=0, concat_axis=0, tiled=True),
                lax.all_to_all(map_sent, "prow", split_axis=0, concat_axis=0, tiled=True),
            )
            records.append((position, block_got, map_got))
            carried = unpack_blocks(values_got, block_got, map_got, width, edge)
    outputs = [None] * levels
    parent = None
    for level in reversed(range(levels)):
        if level == levels - 1:
            values_now = solved[level]
        else:
            factor = panel[level, 0]
            flat = parent.reshape(blocks_dev * edge, nright)

            def back_piece(start, count, factor=factor, flat=flat):
                return lax.dot_general(
                    factor, flat, (((0,), (0,)), ((), ())), preferred_element_type=jnp.float32
                )

            back_here = lax.psum_scatter(
                back_piece(jnp.int32(0), rows_here * lax.axis_size("pcol")),
                "pcol",
                scatter_dimension=0,
                tiled=True,
            )
            values_now = (solved[level].astype(jnp.float32) - back_here).astype(jnp.bfloat16)
        inverse = diag_inv[level, 0]

        def solve_back(start, count, inverse=inverse, values_now=values_now):
            return lax.dot_general(
                inverse, values_now, (((0,), (0,)), ((), ())), preferred_element_type=jnp.float32
            )

        answer = lax.psum_scatter(
            solve_back(jnp.int32(0), rows_here * lax.axis_size("pcol")),
            "pcol",
            scatter_dimension=0,
            tiled=True,
        ).astype(jnp.bfloat16)
        outputs[level] = answer
        if level > 0:
            position, block_got, map_got = records[level - 1]
            owners_here = owner[level - 1, 0, :, 0]
            blocks_here = target_block[level - 1, 0]
            maps_here = row_map[level - 1, 0]
            every = lax.all_gather(answer, ("prow", "pcol"), axis=0, tiled=True)
            index = owners_here[:, None] * width + blocks_here[:, None] * edge + maps_here
            valid = maps_here >= 0
            picked = jnp.take(every, jnp.where(valid, index, 0), axis=0)
            parent = jnp.where(valid[:, :, None], picked, jnp.zeros_like(picked))
    return jnp.stack(outputs)[:, None]


def solution(mesh):
    return jax.shard_map(
        shards,
        mesh=mesh,
        in_specs=(
            P(None, "prow", "pcol", None),
            P(None, "prow", "pcol", None),
            P(None, "prow", "pcol", None),
            P(None, "prow", "pcol", None),
            P(None, "prow", "pcol"),
            P(None, "prow", "pcol", None),
        ),
        out_specs=P(None, "prow", "pcol", None),
        check_vma=False,
    )
```

profile of v0, /device:TPU:1, one launch (start us, length us, event | category | flops | bytes accessed | tf_op | source)
XLA Modules:
  0.0 1501.6 jit_solution(14781600508577444920)
XLA Ops:
  10.2 10.0 all-to-all-start
  22.0 18.9 %all-gather = bf16[1,1,1024,128]{3,2,1,0:T(8,128)(2,1)S(1)} all-gather(bf16[1,1,64,128]{3,2,1,0:T(8,128)(2,1)S(1)} %slice.77), channel_id=2, replica_groups=mesh['prow'=16,'pcol'=16] {'pcol'}, dimensions={2}, use_global_device_ids=true | all-gather | bytes 278528 | tf_op jit(solution)/shard_map/all_gather | solution.py:80
  42.0 17.8 %all_gather.31 = bf16[1024,128]{1,0:T(8,128)(2,1)S(1)} all-gather(bf16[64,128]{1,0:T(8,128)(2,1)S(1)} %convolution_convert_fusion.6), channel_id=1, replica_groups=mesh['prow'=16,'pcol'=16] {'pcol'}, dimensions={0}, use_global_device_ids=true | all-gather | bytes 278528 | tf_op jit(solution)/shard_map/all_gather | solution.py:91
  64.0 17.8 %all-to-all-start.1 = ((s32[16,1,256]{2,1,0:T(1,128)}), s32[16,1,256]{2,1,0:T(1,128)S(1)}, u32[]{:S(2)}, u32[]{:S(2)}) async-start(s32[16,1,256]{2,1,0:T(1,128)} %copy.74), calls=%async_computation.1 | async-start | bytes 32768 | tf_op jit(solution)/shard_map/all_to_all | solution.py:106
  94.4 26.5 %all-to-all-done.2 = bf16[16,256,128]{2,1,0:T(8,128)(2,1)S(1)} async-done(((bf16[16,256,128]{2,1,0:T(8,128)(2,1)}), bf16[16,256,128]{2,1,0:T(8,128)(2,1)S(1)}, u32[]{:S(2)}, u32[]{:S(2)}) %all-to-all-start.2) | async-done | bytes 1048608 | tf_op jit(solution)/shard_map/all_to_all | solution.py:104
  129.7 65.1 %reduce-scatter.19.cloned.1.call-done = f32[64,128]{1,0:T(8,128)} async-done(((f32[1024,128]{1,0:T(8,128)}), f32[64,128]{1,0:T(8,128)}) %reduce-scatter.19.cloned.1.call-update) | async-done | bytes 32784 | tf_op jit(solution)/shard_map/reduce_scatter | solution.py:71
  195.5 17.0 %all_gather.32 = bf16[1024,128]{1,0:T(8,128)(2,1)S(1)} all-gather(bf16[64,128]{1,0:T(8,128)(2,1)S(1)} %fusion.81), channel_id=1, replica_groups=mesh['prow'=16,'pcol'=16] {'pcol'}, dimensions={0}, use_global_device_ids=true | all-gather | bytes 278528 | tf_op jit(solution)/shard_map/all_gather | solution.py:80
  212.7 16.7 %all_gather.33 = bf16[1024,128]{1,0:T(8,128)(2,1)S(1)} all-gather(bf16[64,128]{1,0:T(8,128)(2,1)S(1)} %fusion.54), channel_id=1, replica_groups=mesh['prow'=16,'pcol'=16] {'pcol'}, dimensions={0}, use_global_device_ids=true | all-gather | bytes 278528 | tf_op jit(solution)/shard_map/all_gather | solution.py:91
  233.1 20.3 %all-to-all-start.4 = ((s32[16,1,256]{2,1,0:T(1,128)}), s32[16,1,256]{2,1,0:T(1,128)S(1)}, u32[]{:S(2)}, u32[]{:S(2)}) async-start(s32[16,1,256]{2,1,0:T(1,128)} %copy.82), calls=%async_computation.5 | async-start | bytes 32768 | tf_op jit(solution)/shard_map/all_to_all | solution.py:106
  255.3 5.3 all-to-all-done.4
  265.5 26.9 %all-to-all-done.5 = bf16[16,256,128]{2,1,0:T(8,128)(2,1)S(1)} async-done(((bf16[16,256,128]{2,1,0:T(8,128)(2,1)}), bf16[16,256,128]{2,1,0:T(8,128)(2,1)S(1)}, u32[]{:S(2)}, u32[]{:S(2)}) %all-to-all-start.5) | async-done | bytes 1048608 | tf_op jit(solution)/shard_map/all_to_all | solution.py:104
  301.2 65.6 %reduce-scatter.21.cloned.1.call-done = f32[64,128]{1,0:T(8,128)} async-done(((f32[1024,128]{1,0:T(8,128)}), f32[64,128]{1,0:T(8,128)}) %reduce-scatter.21.cloned.1.call-update) | async-done | bytes 32784 | tf_op jit(solution)/shard_map/reduce_scatter | solution.py:71
  367.5 17.0 %all_gather.34 = bf16[1024,128]{1,0:T(8,128)(2,1)S(1)} all-gather(bf16[64,128]{1,0:T(8,128)(2,1)S(1)} %fusion.80), channel_id=1, replica_groups=mesh['prow'=16,'pcol'=16] {'pcol'}, dimensions={0}, use_global_device_ids=true | all-gather | bytes 278528 | tf_op jit(solution)/shard_map/all_gather | solution.py:80
  384.7 16.7 %all_gather.35 = bf16[1024,128]{1,0:T(8,128)(2,1)S(1)} all-gather(bf16[64,128]{1,0:T(8,128)(2,1)S(1)} %fusion.55), channel_id=1, replica_groups=mesh['prow'=16,'pcol'=16] {'pcol'}, dimensions={0}, use_global_device_ids=true | all-gather | bytes 278528 | tf_op jit(solution)/shard_map/all_gather | solution.py:91
  405.1 20.3 %all-to-all-start.7 = ((s32[16,1,256]{2,1,0:T(1,128)}), s32[16,1,256]{2,1,0:T(1,128)S(1)}, u32[]{:S(2)}, u32[]{:S(2)}) async-start(s32[16,1,256]{2,1,0:T(1,128)} %copy.90), calls=%async_computation.9 | async-start | bytes 32768 | tf_op jit(solution)/shard_map/all_to_all | solution.py:106
  427.4 5.3 all-to-all-done.7
  437.4 27.1 %all-to-all-done.8 = bf16[16,256,128]{2,1,0:T(8,128)(2,1)S(1)} async-done(((bf16[16,256,128]{2,1,0:T(8,128)(2,1)}), bf16[16,256,128]{2,1,0:T(8,128)(2,1)S(1)}, u32[]{:S(2)}, u32[]{:S(2)}) %all-to-all-start.8) | async-done | bytes 1048608 | tf_op jit(solution)/shard_map/all_to_all | solution.py:104
  467.9 71.0 %reduce-scatter.23.cloned.1.call-done = f32[64,128]{1,0:T(8,128)} async-done(((f32[1024,128]{1,0:T(8,128)}), f32[64,128]{1,0:T(8,128)}) %reduce-scatter.23.cloned.1.call-update) | async-done | bytes 32784 | tf_op jit(solution)/shard_map/reduce_scatter | solution.py:71
  539.6 16.9 %all_gather.36 = bf16[1024,128]{1,0:T(8,128)(2,1)S(1)} all-gather(bf16[64,128]{1,0:T(8,128)(2,1)S(1)} %fusion.79), channel_id=1, replica_groups=mesh['prow'=16,'pcol'=16] {'pcol'}, dimensions={0}, use_global_device_ids=true | all-gather | bytes 278528 | tf_op jit(solution)/shard_map/all_gather | solution.py:80
  558.0 82.4 %reduce-scatter.31.cloned.1.call-done = f32[64,128]{1,0:T(8,128)} async-done(((f32[1024,128]{1,0:T(8,128)}), f32[64,128]{1,0:T(8,128)}) %reduce-scatter.31.cloned.1.call-update) | async-done | bytes 32784
  642.4 118.0 %all-gather.5.cloned.1.call-done = bf16[16384,128]{1,0:T(8,128)(2,1)} async-done(((bf16[64,128]{1,0:T(8,128)(2,1)}), bf16[16384,128]{1,0:T(8,128)(2,1)}) %all-gather.5.cloned.1.call-update) | async-done | bytes 4194320 | tf_op jit(solution)/shard_map/all_gather | solution.py:150
  760.4 5.9 gather_fusion
  771.4 72.6 %reduce-scatter.25.cloned.1.call-done = f32[64,128]{1,0:T(8,128)} async-done(((f32[1024,128]{1,0:T(8,128)}), f32[64,128]{1,0:T(8,128)}) %reduce-scatter.25.cloned.1.call-update) | async-done | bytes 32784 | tf_op jit(solution)/shard_map/reduce_scatter | solution.py:124
  846.1 78.5 %reduce-scatter.33.cloned.1.call-done = f32[64,128]{1,0:T(8,128)} async-done(((f32[1024,128]{1,0:T(8,128)}), f32[64,128]{1,0:T(8,128)}) %reduce-scatter.33.cloned.1.call-update) | async-done | bytes 32784
  926.4 118.4 %all-gather.7.cloned.1.call-done = bf16[16384,128]{1,0:T(8,128)(2,1)} async-done(((bf16[64,128]{1,0:T(8,128)(2,1)}), bf16[16384,128]{1,0:T(8,128)(2,1)}) %all-gather.7.cloned.1.call-update) | async-done | bytes 4194320 | tf_op jit(solution)/shard_map/all_gather | solution.py:150
  1044.9 5.9 gather_fusion.1
  1055.9 72.6 %reduce-scatter.27.cloned.1.call-done = f32[64,128]{1,0:T(8,128)} async-done(((f32[1024,128]{1,0:T(8,128)}), f32[64,128]{1,0:T(8,128)}) %reduce-scatter.27.cloned.1.call-update) | async-done | bytes 32784 | tf_op jit(solution)/shard_map/reduce_scatter | solution.py:124
  1130.5 78.4 %reduce-scatter.35.cloned.1.call-done = f32[64,128]{1,0:T(8,128)} async-done(((f32[1024,128]{1,0:T(8,128)}), f32[64,128]{1,0:T(8,128)}) %reduce-scatter.35.cloned.1.call-update) | async-done | bytes 32784
  1210.8 118.4 %all-gather.9.cloned.1.call-done = bf16[16384,128]{1,0:T(8,128)(2,1)} async-done(((bf16[64,128]{1,0:T(8,128)(2,1)}), bf16[16384,128]{1,0:T(8,128)(2,1)}) %all-gather.9.cloned.1.call-update) | async-done | bytes 4194320 | tf_op jit(solution)/shard_map/all_gather | solution.py:150
  1329.2 5.9 gather_fusion.2
  1340.2 72.6 %reduce-scatter.29.cloned.1.call-done = f32[64,128]{1,0:T(8,128)} async-done(((f32[1024,128]{1,0:T(8,128)}), f32[64,128]{1,0:T(8,128)}) %reduce-scatter.29.cloned.1.call-update) | async-done | bytes 32784 | tf_op jit(solution)/shard_map/reduce_scatter | solution.py:124
  1414.8 78.7 %reduce-scatter.37.cloned.1.call-done = f32[64,128]{1,0:T(8,128)} async-done(((f32[1024,128]{1,0:T(8,128)}), f32[64,128]{1,0:T(8,128)}) %reduce-scatter.37.cloned.1.call-update) | async-done | bytes 32784
  (153 shorter events, 97.6 us)
Async XLA Ops:
  10.2 53.8 %all-to-all-start = ((s32[16,1,2]{2,1,0:T(1,128)}), s32[16,1,2]{2,1,0:T(1,128)S(1)}, u32[]{:S(2)}, u32[]{:S(2)}) async-start(s32[16,1,2]{2,1,0:T(1,128)} %bitcast.5), calls=%async_computation | async-start | bytes 16384 | tf_op jit(solution)/shard_map/all_to_all | solution.py:105
  64.0 25.1 %all-to-all-start.1 = ((s32[16,1,256]{2,1,0:T(1,128)}), s32[16,1,256]{2,1,0:T(1,128)S(1)}, u32[]{:S(2)}, u32[]{:S(2)}) async-start(s32[16,1,256]{2,1,0:T(1,128)} %copy.74), calls=%async_computation.1 | async-start | bytes 32768 | tf_op jit(solution)/shard_map/all_to_all | solution.py:106
  89.1 31.8 %all-to-all-start.2 = ((bf16[16,256,128]{2,1,0:T(8,128)(2,1)}), bf16[16,256,128]{2,1,0:T(8,128)(2,1)S(1)}, u32[]{:S(2)}, u32[]{:S(2)}) async-start(bf16[16,256,128]{2,1,0:T(8,128)(2,1)} %bitcast.12), calls=%async_computation.2 | async-start | bytes 2097152 | tf_op jit(solution)/shard_map/all_to_all | solution.py:104
  93.0 101.8 %reduce-scatter.19.cloned.1.call-start = ((), (), s32[]{:S(2)}) async-start(), calls=%async_computation.19 | async-start | bytes 557056 | tf_op jit(solution)/shard_map/reduce_scatter | solution.py:71
  121.0 73.8 %copy-start.1 = (bf16[4,1,64,128]{3,2,1,0:T(8,128)(2,1)S(1)}, bf16[4,1,64,128]{3,2,1,0:T(8,128)(2,1)}, u32[]{:S(2)}) copy-start(bf16[4,1,64,128]{3,2,1,0:T(8,128)(2,1)} %param.8) | copy-start | bytes 196612
  121.0 91.5 %copy-start = (bf16[4,1,64,1024]{3,2,1,0:T(8,128)(2,1)S(1)}, bf16[4,1,64,1024]{3,2,1,0:T(8,128)(2,1)}, u32[]{:S(2)}) copy-start(bf16[4,1,64,1024]{3,2,1,0:T(8,128)(2,1)} %param.9) | copy-start | bytes 1572868
  125.1 107.9 %all-to-all-start.3 = ((s32[16,1,2]{2,1,0:T(1,128)}), s32[16,1,2]{2,1,0:T(1,128)S(1)}, u32[]{:S(2)}, u32[]{:S(2)}) async-start(s32[16,1,2]{2,1,0:T(1,128)} %bitcast.21), calls=%async_computation.4 | async-start | bytes 16384 | tf_op jit(solution)/shard_map/all_to_all | solution.py:105
  233.1 27.6 %all-to-all-start.4 = ((s32[16,1,256]{2,1,0:T(1,128)}), s32[16,1,256]{2,1,0:T(1,128)S(1)}, u32[]{:S(2)}, u32[]{:S(2)}) async-start(s32[16,1,256]{2,1,0:T(1,128)} %copy.82), calls=%async_computation.5 | async-start | bytes 32768 | tf_op jit(solution)/shard_map/all_to_all | solution.py:106
  260.7 31.8 %all-to-all-start.5 = ((bf16[16,256,128]{2,1,0:T(8,128)(2,1)}), bf16[16,256,128]{2,1,0:T(8,128)(2,1)S(1)}, u32[]{:S(2)}, u32[]{:S(2)}) async-start(bf16[16,256,128]{2,1,0:T(8,128)(2,1)} %bitcast.28), calls=%async_computation.6 | async-start | bytes 2097152 | tf_op jit(solution)/shard_map/all_to_all | solution.py:104
  264.5 102.3 %reduce-scatter.21.cloned.1.call-start = ((), (), s32[]{:S(2)}) async-start(), calls=%async_computation.20 | async-start | bytes 557056 | tf_op jit(solution)/shard_map/reduce_scatter | solution.py:71
  296.7 108.4 %all-to-all-start.6 = ((s32[16,1,2]{2,1,0:T(1,128)}), s32[16,1,2]{2,1,0:T(1,128)S(1)}, u32[]{:S(2)}, u32[]{:S(2)}) async-start(s32[16,1,2]{2,1,0:T(1,128)} %bitcast.37), calls=%async_computation.8 | async-start | bytes 16384 | tf_op jit(solution)/shard_map/all_to_all | solution.py:105
  405.1 27.6 %all-to-all-start.7 = ((s32[16,1,256]{2,1,0:T(1,128)}), s32[16,1,256]{2,1,0:T(1,128)S(1)}, u32[]{:S(2)}, u32[]{:S(2)}) async-start(s32[16,1,256]{2,1,0:T(1,128)} %copy.90), calls=%async_computation.9 | async-start | bytes 32768 | tf_op jit(solution)/shard_map/all_to_all | solution.py:106
  432.7 31.8 %all-to-all-start.8 = ((bf16[16,256,128]{2,1,0:T(8,128)(2,1)}), bf16[16,256,128]{2,1,0:T(8,128)(2,1)S(1)}, u32[]{:S(2)}, u32[]{:S(2)}) async-start(bf16[16,256,128]{2,1,0:T(8,128)(2,1)} %bitcast.44), calls=%async_computation.10 | async-start | bytes 2097152 | tf_op jit(solution)/shard_map/all_to_all | solution.py:104
  436.5 102.3 %reduce-scatter.23.cloned.1.call-start = ((), (), s32[]{:S(2)}) async-start(), calls=%async_computation.21 | async-start | bytes 557056 | tf_op jit(solution)/shard_map/reduce_scatter | solution.py:71
  467.8 172.5 %reduce-scatter.31.cloned.1.call-start = ((), (), s32[]{:S(2)}) async-start(), calls=%async_computation.28 | async-start | bytes 557056
  558.0 202.4 %all-gather.5.cloned.1.call-start = ((), (), s32[]{:S(2)}) async-start(), calls=%async_computation.22 | async-start | bytes 4210688 | tf_op jit(solution)/shard_map/all_gather | solution.py:150
  642.0 202.1 %reduce-scatter.25.cloned.1.call-start = ((), (), s32[]{:S(2)}) async-start(), calls=%async_computation.23 | async-start | bytes 557056 | tf_op jit(solution)/shard_map/reduce_scatter | solution.py:124
  771.4 153.2 %reduce-scatter.33.cloned.1.call-start = ((), (), s32[]{:S(2)}) async-start(), calls=%async_computation.29 | async-start | bytes 557056
  846.0 198.8 %all-gather.7.cloned.1.call-start = ((), (), s32[]{:S(2)}) async-start(), calls=%async_computation.24 | async-start | bytes 4210688 | tf_op jit(solution)/shard_map/all_gather | solution.py:150
  926.2 202.2 %reduce-scatter.27.cloned.1.call-start = ((), (), s32[]{:S(2)}) async-start(), calls=%async_computation.25 | async-start | bytes 557056 | tf_op jit(solution)/shard_map/reduce_scatter | solution.py:124
  1055.8 153.1 %reduce-scatter.35.cloned.1.call-start = ((), (), s32[]{:S(2)}) async-start(), calls=%async_computation.30 | async-start | bytes 557056
  1130.5 198.7 %all-gather.9.cloned.1.call-start = ((), (), s32[]{:S(2)}) async-start(), calls=%async_computation.26 | async-start | bytes 4210688 | tf_op jit(solution)/shard_map/all_gather | solution.py:150
  1210.6 202.2 %reduce-scatter.29.cloned.1.call-start = ((), (), s32[]{:S(2)}) async-start(), calls=%async_computation.27 | async-start | bytes 557056 | tf_op jit(solution)/shard_map/reduce_scatter | solution.py:124
  1340.1 153.3 %reduce-scatter.37.cloned.1.call-start = ((), (), s32[]{:S(2)}) async-start(), calls=%async_computation.31 | async-start | bytes 557056
Sparse Core Ops, SparseCore 0:
  124.4 70.3 reduce-scatter.18
  295.9 70.8 reduce-scatter.20
  467.9 70.8 reduce-scatter.22
  558.1 82.2 reduce-scatter.30
  643.8 116.5 all-gather.4
  771.5 72.4 reduce-scatter.24
  847.9 76.6 reduce-scatter.32
  928.2 116.6 all-gather.6
  1056.0 72.4 reduce-scatter.26
  1132.2 76.7 reduce-scatter.34
  1212.5 116.5 all-gather.8
  1340.2 72.4 reduce-scatter.28
  1416.6 76.7 reduce-scatter.36
where the time goes:
time: 1500 us
  waiting for transfers between devices  1190 us (79%)
  blocking collectives  121 us (8%)
  starting transfers between devices  87.8 us (6%)
  local copies, waits for them, and re-layouts  43.8 us (3%)
  matrix products  37.1 us (2%)
    all_gather x3, waiting for transfers between devices, shards(): every = lax.all_gather(answer, ('prow', 'pcol'), axis=0, tiled=True)  355 us
    unnamed x17, waiting for transfers between devices  318 us
    reduce_scatter x3, waiting for transfers between devices, shards(): lax.psum_scatter(back_piece(jnp.int32(0), rows_here * lax.axis_size('pcol...  218 us
    reduce_scatter x3, waiting for transfers between devices, shards(): lax.psum_scatter(carried, 'pcol', scatter_dimension=0, tiled=True)  202 us
    all_to_all x3, waiting for transfers between devices, shards(): lax.all_to_all(values, 'prow', split_axis=0, concat_axis=0, tiled=True)  80.6 us
    all_gather x4, blocking collectives, shards(): lax.all_gather(rights, 'pcol', axis=0, tiled=True)  69.7 us
    all_to_all x3, starting transfers between devices, shards(): lax.all_to_all(map_sent, 'prow', split_axis=0, concat_axis=0, tiled=True)  58.3 us
    all_gather x3, blocking collectives, shards(): lax.all_gather(solved_here, 'pcol', axis=0, tiled=True)  51.2 us
  transfers between devices with their start and end apart: 22, of which 19 were waited for; matrix products, arithmetic and copies ran while one was open for 2% of the time, Pallas kernels for 0%

commit v1 on v0

v1 whole, which is shorter than its diff:
```python
import functools

import jax
import jax.numpy as jnp
from jax import lax
from jax.experimental import pallas as pl
from jax.experimental.pallas import tpu as pltpu
from jax.sharding import PartitionSpec as P

MESH = pl.DeviceIdType.MESH
N = 16
F32 = jnp.float32
BF16 = jnp.bfloat16


def nt(a, b):
    return lax.dot_general(a, b, (((1,), (1,)), ((), ())), preferred_element_type=F32)


def nn(a, b):
    return jnp.dot(a, b, preferred_element_type=F32)


S_C0, S_Y0, S_V, S_R, S_F1, S_F2, S_F3, S_B1, S_B2, S_B3, S_OUT, S_X0 = (
    0, 1, 2, 3, 4, 7, 10, 13, 16, 19, 22, 25)
NSEM = 26


def kernel(rhs, dinv, panel_hbm, vcode, rmap, out,
           panel, dfull, emat, c0, y0, sr, rr, rhsc, vall, yt, ct,
           s1, r1, s2, r2, s3, r3, sb1, rb1, s4, r4, gt, tt, wt, s5, r5, so, ro, s7, r7, xf, tile,
           psem, ssem, rsem, dss, drs):
    p = lax.axis_index("prow")
    c = lax.axis_index("pcol")
    x, y = c // 4, c % 4

    def plane_dev(d):
        return (p, lax.rem(x + d // 4, 4) * 4 + lax.rem(y + d % 4, 4))

    def col_dev(d):
        return (lax.rem(p + d, N), c)

    for l in range(3):
        pltpu.make_async_copy(panel_hbm.at[l], panel.at[l], psem.at[l]).start()

    bar = pltpu.get_barrier_semaphore()

    def greet(d, _):
        pl.semaphore_signal(bar, inc=1, device_id=plane_dev(d), device_id_type=MESH)
        pl.semaphore_signal(bar, inc=1, device_id=col_dev(d), device_id_type=MESH)
        return 0

    c0[c] = rhs[0]
    vall[c] = vcode[...]
    r1[:, :, 112:128, :] = jnp.zeros((3, N, 16, 128), BF16)
    lax.fori_loop(1, N, greet, 0)
    pl.semaphore_wait(bar, 30)

    def spread(dev, src, dst, sem):
        def step(d, _):
            to = dev(d)
            pltpu.make_async_remote_copy(src(to), dst, ssem.at[sem], rsem.at[sem], device_id=to, device_id_type=MESH).start()
            return 0
        lax.fori_loop(1, N, step, 0)

    def wait_all(ref, sem):
        pltpu.make_async_copy(ref, ref, sem).wait()

    spread(plane_dev, lambda to: c0.at[c], c0.at[c], S_C0)
    spread(plane_dev, lambda to: vall.at[c], vall.at[c], S_V)
    for l in range(0, 4, 2):
        halves = []
        for k in (l, l + 1):
            r = rhs[k].astype(F32)
            halves.append(jnp.concatenate([r, r], axis=0).T.reshape(N, 8, 128))
        sr[:, l * 8:l * 8 + 16, :] = jnp.concatenate(halves, axis=1).astype(BF16)
    rr[c] = sr[c]
    spread(plane_dev, lambda to: sr.at[to[1]], rr.at[c], S_R)
    wait_all(c0.at[pl.ds(0, 15)], rsem.at[S_C0])
    y0[c] = nn(dinv[0], c0[...].reshape(1024, 128)).astype(BF16)
    spread(plane_dev, lambda to: y0.at[c], y0.at[c], S_Y0)

    wait_all(rr.at[pl.ds(0, 15)], rsem.at[S_R])
    first = lax.broadcasted_iota(jnp.int32, (8, 128), 1) < 64
    for l in range(1, 4):
        for tb in range(8):
            a = rr[2 * tb, :, :].astype(F32)[8 * l:8 * l + 8]
            b = rr[2 * tb + 1, :, :].astype(F32)[8 * l:8 * l + 8]
            rhsc[l, tb * 8:tb * 8 + 8, :] = jnp.where(first, a, b)
    wait_all(vall.at[pl.ds(0, 15)], rsem.at[S_V])

    def build_e(l):
        rows = lax.broadcasted_iota(jnp.int32, (1024, 128), 0)

        def one(s, _):
            v = vall[s, pl.ds(l, 1), :]
            emat[:, pl.ds(pl.multiple_of(s * 128, 128), 128)] = jnp.where(rows == v, 1.0, 0.0).astype(BF16)
            return 0
        lax.fori_loop(0, N, one, 0)

    def build_et(l, ematt):
        lanes = lax.broadcasted_iota(jnp.int32, (128, 1024), 1).astype(F32)

        def one(s, _):
            v = jnp.broadcast_to(vall[s, pl.ds(l, 1), :].astype(F32), (128, 128)).T
            v = jnp.concatenate([v] * 8, axis=1)
            ematt[pl.ds(pl.multiple_of(s * 128, 128), 128), :] = jnp.where(lanes == v, 1.0, 0.0).astype(BF16)
            return 0
        lax.fori_loop(0, N, one, 0)

    def d_tile(l, m, rows):
        return dfull.at[l, rows, pl.ds(m * 256, 256)]

    def start_d(l):
        mine = pl.ds(pl.multiple_of(c * 64, 64), 64)
        dfull[l, mine, :] = dinv[l]
        for m in range(4):
            @pl.when(c >= 4 * m)
            def _():
                def step(d, _):
                    pltpu.make_async_remote_copy(
                        dinv.at[l, :, pl.ds(m * 256, 256)], d_tile(l, m, mine), dss.at[l, m], drs.at[l, m],
                        device_id=plane_dev(d), device_id_type=MESH).start()
                    return 0
                lax.fori_loop(1, N, step, 0)

    def wait_d(l):
        for m in range(4):
            n = 16 - 4 * m

            @pl.when(c >= 4 * m)
            def _():
                wait_all(d_tile(l, m, pl.ds(0, 64 * (n - 1))), drs.at[l, m])

            @pl.when(c < 4 * m)
            def _():
                wait_all(d_tile(l, m, pl.ds(0, 64 * n)), drs.at[l, m])

    def place(l, b):
        rows = lax.broadcasted_iota(jnp.int32, (128, 128), 0)
        return jnp.where(rows == rmap[l, pl.ds(b, 1), :], 1.0, 0.0).astype(BF16)

    wait_all(y0.at[pl.ds(0, 15)], rsem.at[S_Y0])
    for i in range(8):
        yt[0, :, i * 128:i * 128 + 128] = y0[2 * i:2 * i + 2].reshape(128, 128).astype(F32).T.astype(BF16)

    def forward(l, _):
        pltpu.make_async_copy(panel_hbm.at[l], panel.at[l], psem.at[l]).wait()

        def pair(n, _):
            u = nt(yt[l], panel[l, pl.ds(pl.multiple_of(n * 256, 256), 256), :]).astype(BF16)
            a = nt(u[:, :128], place(l, 2 * n)).reshape(N, 8, 128)
            b = nt(u[:, 128:], place(l, 2 * n + 1)).reshape(N, 8, 128)
            s1[l, :, pl.ds(pl.multiple_of(n * 16, 16), 16), :] = jnp.concatenate([a, b], axis=1).astype(BF16)
            return 0
        lax.fori_loop(0, 7, pair, 0)
        r1[l, c, 0:112, :] = s1[l, c]
        spread(plane_dev, lambda to: s1.at[l, to[1]], r1.at[l, c, pl.ds(0, 112), :], S_F1 + l)
        build_e(l)
        start_d(l + 1)
        wait_all(r1.at[l, pl.ds(0, 15), pl.ds(0, 112), :], rsem.at[S_F1 + l])

        def owners(n, _):
            rows = nn(emat[pl.ds(pl.multiple_of(n * 256, 256), 256), :], r1[l].reshape(2048, 128))
            s2[l, pl.ds(n * 4, 4)] = rows.astype(BF16).reshape(4, 64, 128)
            return 0
        lax.fori_loop(0, 4, owners, 0)
        r2[l, p] = s2[l, p]
        spread(col_dev, lambda to: s2.at[l, to[0]], r2.at[l, p], S_F2 + l)
        wait_all(r2.at[l, pl.ds(0, 15)], rsem.at[S_F2 + l])
        carried = jnp.sum(r2[l].astype(F32), axis=0)
        s3[l] = (rhsc[l + 1] - carried).astype(BF16)
        r3[l, c] = s3[l]
        spread(plane_dev, lambda to: s3.at[l], r3.at[l, c], S_F3 + l)
        wait_all(r3.at[l, pl.ds(0, 15)], rsem.at[S_F3 + l])
        got = r3[l].astype(F32).reshape(N, 8, 8, 128)
        for tb in range(8):
            ct[:, tb * 128:tb * 128 + 128] = got[:, tb].reshape(128, 128).astype(BF16)
        wait_d(l + 1)
        for i in range(4):
            k = 256 * (i + 1)
            yt[l + 1, :, i * 256:k] = nt(ct[:, :k], dfull[l + 1, i * 256:k, :k]).astype(BF16)
        return 0

    lax.fori_loop(0, 3, forward, 0)

    def back_solve(l):
        for m in range(4):
            xf[:, m * 256:m * 256 + 256] = nn(wt[:, m * 256:], dfull[l, m * 256:, m * 256:m * 256 + 256])

    def my_rows(tile_value):
        tile[...] = tile_value.T
        return tile[pl.ds(pl.multiple_of(lax.rem(c, 2) * 64, 64), 64), :].astype(BF16)

    wt[...] = yt[3]
    back_solve(3)
    mine8 = pl.ds(pl.multiple_of(c * 8, 8), 8)
    for tb in range(0, 8, 2):
        sb1[2, tb * 8:tb * 8 + 16, :] = jnp.concatenate(
            [xf[mine8, tb * 128:tb * 128 + 128], xf[mine8, tb * 128 + 128:tb * 128 + 256]], axis=0).astype(BF16)
    my_tile = c // 2

    def backward_to_partials(l):
        rb1[l, p] = sb1[l]
        spread(col_dev, lambda to: sb1.at[l], rb1.at[l, p], S_B1 + l)
        build_et(l, ematt=emat_t)
        wait_all(rb1.at[l, pl.ds(0, 15)], rsem.at[S_B1 + l])

        def holders(n, _):
            rows = nn(emat_t[pl.ds(pl.multiple_of(n * 256, 256), 256), :], rb1[l].reshape(1024, 128))
            s4[l, pl.ds(n * 2, 2)] = rows.astype(BF16).reshape(2, 128, 128)
            return 0
        lax.fori_loop(0, 8, holders, 0)
        r4[l, c] = s4[l, c, 0:112, :]
        spread(plane_dev, lambda to: s4.at[l, to[1], pl.ds(0, 112), :], r4.at[l, c], S_B2 + l)

    def backward_rest(l):
        wait_all(r4.at[l, pl.ds(0, 15)], rsem.at[S_B2 + l])

        def pair(n, _):
            got = r4[l, :, pl.ds(pl.multiple_of(n * 16, 16), 16), :].astype(F32)
            a = nn(got[:, :8].reshape(128, 128).astype(BF16), place(l, 2 * n))
            b = nn(got[:, 8:].reshape(128, 128).astype(BF16), place(l, 2 * n + 1))
            gt[:, pl.ds(pl.multiple_of(n * 256, 256), 256)] = jnp.concatenate([a, b], axis=1).astype(BF16)
            return 0
        lax.fori_loop(0, 7, pair, 0)

        def columns(n, _):
            cols = pl.ds(pl.multiple_of(n * 256, 256), 256)
            t = nn(gt[...], panel[l, :, cols])
            wt[:, cols] = (yt[l, :, cols].astype(F32) * (1.0 / 16) - t).astype(BF16)
            return 0
        lax.fori_loop(0, 4, columns, 0)
        back_solve(l)

    emat_t = tt

    def backward(m, _):
        l = 2 - m
        backward_to_partials(l)

        @pl.when(m == 0)
        def _():
            start_d(0)
        backward_rest(l)
        for tb in range(0, 8, 2):
            a = xf[:, tb * 128:tb * 128 + 128].reshape(N, 8, 128)
            b = xf[:, tb * 128 + 128:tb * 128 + 256].reshape(N, 8, 128)
            s5[l, :, tb * 8:tb * 8 + 16, :] = jnp.concatenate([a, b], axis=1).astype(BF16)
        r5[l, c] = s5[l, c]
        spread(plane_dev, lambda to: s5.at[l, to[1]], r5.at[l, c], S_B3 + l)
        wait_all(r5.at[l, pl.ds(0, 15)], rsem.at[S_B3 + l])
        total = jnp.sum(r5[l].astype(F32), axis=0).astype(BF16)
        sb1[l - 1] = total
        so[l] = total.astype(F32).reshape(8, 8, 128)
        ro[l, c] = so[l, my_tile]
        spread(plane_dev, lambda to: so.at[l, to[1] // 2], ro.at[l, c], S_OUT + l)
        return 0

    out[3] = my_rows(xf[:, pl.ds(pl.multiple_of(my_tile * 128, 128), 128)])
    lax.fori_loop(0, 2, backward, 0)
    backward_to_partials(0)
    for l in (2, 1):
        wait_all(ro.at[l, pl.ds(0, 15)], rsem.at[S_OUT + l])
        out[l] = my_rows(ro[l].reshape(128, 128))
    wait_d(0)
    backward_rest(0)
    for i in range(8):
        s7[2 * i:2 * i + 2] = xf[:, i * 128:i * 128 + 128].T.astype(BF16).reshape(2, 64, 128)
    r7[c] = s7[c]
    spread(plane_dev, lambda to: s7.at[to[1]], r7.at[c], S_X0)
    wait_all(r7.at[pl.ds(0, 15)], rsem.at[S_X0])
    out[0] = jnp.sum(r7[...].astype(F32), axis=0).astype(BF16)

    wait_all(c0.at[pl.ds(0, 15)], ssem.at[S_C0])
    wait_all(y0.at[pl.ds(0, 15)], ssem.at[S_Y0])
    wait_all(vall.at[pl.ds(0, 15)], ssem.at[S_V])
    wait_all(rr.at[pl.ds(0, 15)], ssem.at[S_R])
    wait_all(r7.at[pl.ds(0, 15)], ssem.at[S_X0])
    for l in range(3):
        wait_all(s1.at[l, pl.ds(0, 15)], ssem.at[S_F1 + l])
        wait_all(s2.at[l, pl.ds(0, 15)], ssem.at[S_F2 + l])
        wait_all(r3.at[l, pl.ds(0, 15)], ssem.at[S_F3 + l])
        wait_all(rb1.at[l, pl.ds(0, 15)], ssem.at[S_B1 + l])
        wait_all(r4.at[l, pl.ds(0, 15)], ssem.at[S_B2 + l])
        if l > 0:
            wait_all(s5.at[l, pl.ds(0, 15)], ssem.at[S_B3 + l])
            wait_all(ro.at[l, pl.ds(0, 15)], ssem.at[S_OUT + l])
    for l in range(4):
        for m in range(4):
            @pl.when(c >= 4 * m)
            def _():
                wait_all(d_tile(l, m, pl.ds(0, 64 * 15)), dss.at[l, m])


def shards(rhs, diag_inv, panel, owner, target_block, row_map):
    code = (owner[:, 0, :, 0] * 8 + target_block[:, 0])[:, :, None] * 8 + jnp.arange(8, dtype=jnp.int32)
    code = jnp.pad(code.reshape(3, 112), ((0, 5), (0, 16)), constant_values=-1)
    vm = pl.BlockSpec(memory_space=pltpu.VMEM)
    b = lambda *s: pltpu.VMEM(s, BF16)
    f = lambda *s: pltpu.VMEM(s, F32)
    scratch = [
        b(3, 1792, 1024),
        b(4, 1024, 1024),
        b(1024, 2048),
        b(16, 64, 128), b(16, 64, 128),
        b(16, 32, 128), b(16, 32, 128), f(4, 64, 128),
        pltpu.VMEM((16, 8, 128), jnp.int32),
        b(4, 128, 1024), b(128, 1024),
        b(3, 16, 112, 128), b(3, 16, 128, 128),
        b(3, 16, 64, 128), b(3, 16, 64, 128),
        b(3, 64, 128), b(3, 16, 64, 128),
        b(3, 64, 128), b(3, 16, 64, 128),
        b(3, 16, 128, 128), b(3, 16, 112, 128),
        b(128, 1792), b(2048, 1024), b(128, 1024),
        b(3, 16, 64, 128), b(3, 16, 64, 128),
        f(3, 8, 8, 128), f(3, 16, 8, 128),
        b(16, 64, 128), b(16, 64, 128),
        f(128, 1024), f(128, 128),
        pltpu.SemaphoreType.DMA((3,)), pltpu.SemaphoreType.DMA((NSEM,)), pltpu.SemaphoreType.DMA((NSEM,)),
        pltpu.SemaphoreType.DMA((4, 4)), pltpu.SemaphoreType.DMA((4, 4)),
    ]
    got = pl.pallas_call(
        kernel,
        out_shape=jax.ShapeDtypeStruct((4, 64, 128), BF16),
        in_specs=[vm, vm, pl.BlockSpec(memory_space=pl.ANY), vm, vm],
        out_specs=vm,
        scratch_shapes=scratch,
        compiler_params=pltpu.CompilerParams(
            collective_id=0, has_side_effects=True, vmem_limit_bytes=58 << 20),
    )(rhs[:, 0], diag_inv[:, 0], panel[:, 0], code, row_map[:, 0])
    return got[:, None]


def solution(mesh):
    return jax.shard_map(
        shards,
        mesh=mesh,
        in_specs=(
            P(None, "prow", "pcol", None),
            P(None, "prow", "pcol", None),
            P(None, "prow", "pcol", None),
            P(None, "prow", "pcol", None),
            P(None, "prow", "pcol"),
            P(None, "prow", "pcol", None),
        ),
        out_specs=P(None, "prow", "pcol", None),
        check_vma=False,
    )
```

time: 1500 us -> 228 us (0.15)
  waiting for transfers between devices: 1190 us -> 0 us
  Pallas kernels: 0 us -> 222 us
  blocking collectives: 121 us -> 0 us
  starting transfers between devices: 87.8 us -> 0 us
  local copies, waits for them, and re-layouts: 43.8 us -> 3.66 us
  matrix products: 37.1 us -> 0 us
    reduce_scatter x6 -> x0, waiting for transfers between devices: 419 us -> none  [the longest x3 218 us: shards(): lax.psum_scatter(back_piece(jnp.int32(0), rows_here * lax.axis_size('pcol...]
    all_gather x3 -> x0, waiting for transfers between devices: 355 us -> none  [shards(): every = lax.all_gather(answer, ('prow', 'pcol'), axis=0, tiled=True)]
    unnamed x17 -> x0, waiting for transfers between devices: 318 us -> none
    pallas_call x0 -> x1, Pallas kernels: none -> 222 us  [shards(): pl.pallas_call(kernel, out_shape=jax.ShapeDtypeStruct((4, 64, 128), BF16)...]
    all_gather x7 -> x0, blocking collectives: 121 us -> none  [the longest x4 69.7 us: shards(): lax.all_gather(rights, 'pcol', axis=0, tiled=True)]
    all_to_all x9 -> x0, waiting for transfers between devices: 96.6 us -> none  [the longest x3 80.6 us: shards(): lax.all_to_all(values, 'prow', split_axis=0, concat_axis=0, tiled=True)]
    all_to_all x9 -> x0, starting transfers between devices: 86.8 us -> none  [the longest x3 58.3 us: shards(): lax.all_to_all(map_sent, 'prow', split_axis=0, concat_axis=0, tiled=True)]
    dot_general x22 -> x0, matrix products: 37.1 us -> none  [the longest x3 13.1 us: back_piece(): lax.dot_general(factor, flat, (((0,), (0,)), ((), ())), preferred_element...]
  transfers between devices with their start and end apart: 22 -> 0, of which waited for: 19 -> 0; matrix products, arithmetic and copies ran while one was open for 2% -> 0% of each run, Pallas kernels for 0% -> 0%
where the time goes in v1:
time: 228 us; the launch traced here: 227 us
  Pallas kernels  222 us (97%)
  local copies, waits for them, and re-layouts  3.66 us (2%)
    pallas_call x1, Pallas kernels, shards(): pl.pallas_call(kernel, out_shape=jax.ShapeDtypeStruct((4, 64, 128), BF16)...  222 us

profile of v1, /device:TPU:1, one launch (start us, length us, event | category | flops | bytes accessed | tf_op | source)
XLA Modules:
  0.0 227.3 jit_solution(16178216792772347435)
XLA Ops:
  0.0 0.7 broadcast_multiply_fusion
  0.7 0.7 fusion
  1.4 0.1 add.33
  1.5 0.1 add.30
  1.5 0.1 add.31
  1.6 0.6 pad.4.vcode
  2.2 1.3 copy.15
  3.6 222.3 %shard_map.64 = bf16[4,64,128]{2,1,0:T(8,128)(2,1)} custom-call(bf16[4,64,128]{2,1,0:T(8,128)(2,1)} %bitcast.19, bf16[4,64,1024]{2,1,0:T(8,128)(2,1)} %bitcast.16, bf16[3,1792,1024]{2,1,0:T(8,128)(2,1)} %bitcast.15, s32[8,128]{1,0:T(8,128)} %pad.4.vcode, s32[3,14,128]{2,1,0:T(8,128)} %bitcast.18), custom_call_target="tpu_custom_call" | custom-call | tf_op jit(solution)/shard_map/pallas_call | solution.py:323
  225.9 1.5 copy.17
  (2 shorter events, 0.0 us)

commit v2 on v1

v2 whole, which is shorter than its diff:
```python
import functools

import jax
import jax.numpy as jnp
from jax import lax
from jax.experimental import pallas as pl
from jax.experimental.pallas import tpu as pltpu
from jax.sharding import PartitionSpec as P

MESH = pl.DeviceIdType.MESH
N = 16
F32 = jnp.float32
BF16 = jnp.bfloat16


def nt(a, b):
    return lax.dot_general(a, b, (((1,), (1,)), ((), ())), preferred_element_type=F32)


def nn(a, b):
    return jnp.dot(a, b, preferred_element_type=F32)


S_C0, S_Y0, S_V, S_R, S_F1, S_F2, S_F3, S_B1, S_B2, S_B3, S_OUT, S_X0, S_G1, S_FS, S_BS = (
    0, 1, 2, 3, 4, 7, 10, 13, 16, 19, 22, 25, 26, 29, 32)
NSEM = 35


def kernel(rhs, dinv, panel_hbm, owner, tblock, rmap, out,
           panel, dfull, emat, c0, y0, sr, rr, rhsc, vall, yt, ct,
           s1, r1, s2, r2, s3, r3, sb1, rb1, s4, r4, gt, tt, wt, s5, r5, so, ro, s7, r7, xf, tile, wide, half, rsib, rbs, gacc,
           psem, ssem, rsem, dss, drs):
    p = lax.axis_index("prow")
    c = lax.axis_index("pcol")
    x, y = c // 4, c % 4

    def plane_dev(d):
        return (p, lax.rem(x + d // 4, 4) * 4 + lax.rem(y + d % 4, 4))

    z, k = p // 2, lax.rem(p, 2)
    sibling = (z * 2 + 1 - k, c)

    def z_dev(d):
        return (lax.rem(z + d, 8) * 2 + k, c)

    for l in range(3):
        pltpu.make_async_copy(panel_hbm.at[l], panel.at[l], psem.at[l]).start()

    bar = pltpu.get_barrier_semaphore()

    def greet(d, _):
        pl.semaphore_signal(bar, inc=1, device_id=plane_dev(d), device_id_type=MESH)
        return 0

    def greet_z(d, _):
        pl.semaphore_signal(bar, inc=1, device_id=z_dev(d), device_id_type=MESH)
        return 0

    c0[c] = rhs[0]
    r1[:, :, 112:128, :] = jnp.zeros((3, N, 16, 128), BF16)
    lax.fori_loop(1, N, greet, 0)
    lax.fori_loop(1, 8, greet_z, 0)
    pl.semaphore_signal(bar, inc=1, device_id=sibling, device_id_type=MESH)

    own = owner[:, 0, :]
    number = ((lax.rem(own, 2) * 8 + own // 2) * 8 + tblock[:, 0, :]).astype(F32)
    wide[...] = jnp.zeros((8, 128), F32)
    wide[0:3, 0:14] = number
    lane = lax.broadcasted_iota(jnp.int32, (8, 128), 1)
    repeat = (lax.broadcasted_iota(jnp.int32, (128, 128), 1) // 8 == lax.broadcasted_iota(jnp.int32, (128, 128), 0))
    repeated = nn(wide[...].astype(BF16), jnp.where(repeat, 1.0, 0.0).astype(BF16)).astype(jnp.int32)
    vall[c] = jnp.where(lane < 112, repeated * 8 + lax.rem(lane, 8), -1)
    for l in range(0, 4, 2):
        halves = []
        for q in (l, l + 1):
            r = rhs[q].astype(F32)
            halves.append(jnp.concatenate([r, r], axis=0).T.reshape(N, 8, 128))
        sr[:, l * 8:l * 8 + 16, :] = jnp.concatenate(halves, axis=1).astype(BF16)
    rr[c] = sr[c]
    pl.semaphore_wait(bar, 23)

    def spread(dev, src, dst, sem, count=N):
        def step(d, _):
            to = dev(d)
            pltpu.make_async_remote_copy(src(to), dst, ssem.at[sem], rsem.at[sem], device_id=to, device_id_type=MESH).start()
            return 0
        lax.fori_loop(1, count, step, 0)

    def remote(src, dst, to, sem):
        return pltpu.make_async_remote_copy(src, dst, ssem.at[sem], rsem.at[sem], device_id=to, device_id_type=MESH)

    def wait_all(ref, sem):
        pltpu.make_async_copy(ref, ref, sem).wait()

    spread(plane_dev, lambda to: c0.at[c], c0.at[c], S_C0)
    spread(plane_dev, lambda to: vall.at[c], vall.at[c], S_V)
    spread(plane_dev, lambda to: sr.at[to[1]], rr.at[c], S_R)
    wait_all(c0.at[pl.ds(0, 15)], rsem.at[S_C0])
    y0[c] = nn(dinv[0], c0[...].reshape(1024, 128)).astype(BF16)
    spread(plane_dev, lambda to: y0.at[c], y0.at[c], S_Y0)

    wait_all(rr.at[pl.ds(0, 15)], rsem.at[S_R])
    first = lax.broadcasted_iota(jnp.int32, (8, 128), 1) < 64
    for l in range(1, 4):
        for tb in range(8):
            a = rr[2 * tb, :, :].astype(F32)[8 * l:8 * l + 8]
            b = rr[2 * tb + 1, :, :].astype(F32)[8 * l:8 * l + 8]
            rhsc[l, tb * 8:tb * 8 + 8, :] = jnp.where(first, a, b)
    wait_all(vall.at[pl.ds(0, 15)], rsem.at[S_V])

    def build_e(l):
        rows = lax.broadcasted_iota(jnp.int32, (1024, 128), 0)

        def one(s, _):
            v = vall[s, pl.ds(l, 1), :]
            emat[:, pl.ds(pl.multiple_of(s * 128, 128), 128)] = jnp.where(rows == v, 1.0, 0.0).astype(BF16)
            return 0
        lax.fori_loop(0, N, one, 0)

    def build_et(l, ematt):
        lanes = lax.broadcasted_iota(jnp.int32, (128, 1024), 1).astype(F32)

        def one(s, _):
            v = jnp.broadcast_to(vall[s, pl.ds(l, 1), :].astype(F32), (128, 128)).T
            v = jnp.concatenate([v] * 8, axis=1)
            ematt[pl.ds(pl.multiple_of(s * 128, 128), 128), :] = jnp.where(lanes == v, 1.0, 0.0).astype(BF16)
            return 0
        lax.fori_loop(0, N, one, 0)

    def d_tile(l, m, rows):
        return dfull.at[l, m, rows, :]

    def x_dev(d):
        return (p, lax.rem(x + d, 4) * 4 + y)

    def y_dev(d):
        return (p, x * 4 + lax.rem(y + d, 4))

    def send_tile(l, leg, m, dev, rows):
        def step(d, _):
            pltpu.make_async_remote_copy(
                d_tile(l, m, rows), d_tile(l, m, rows), dss.at[l, leg * 4 + m], drs.at[l, leg * 4 + m],
                device_id=dev(d), device_id_type=MESH).start()
            return 0
        lax.fori_loop(1, 4, step, 0)

    def wait_tiles(sems, l, leg, m, tiles):
        wait_all(d_tile(l, m, pl.ds(0, 64 * tiles)), sems.at[l, leg * 4 + m])

    def start_d(l):
        mine = pl.ds(pl.multiple_of(c * 64, 64), 64)
        for m in range(4):
            dfull[l, m, mine, :] = dinv[l, :, m * 256:m * 256 + 256]
        for m, dev in ((0, x_dev), (1, y_dev), (2, y_dev), (3, x_dev)):
            @pl.when(x >= m)
            def _():
                send_tile(l, 0, m, dev, mine)

    def forward_d(l):
        wait_tiles(drs, l, 0, 0, 3)

        @pl.when(x < 3)
        def _():
            wait_tiles(drs, l, 0, 3, 1)

        def chunk(g, _):
            send_tile(l, 1, 0, y_dev, pl.ds(pl.multiple_of((g * 4 + y) * 64, 64), 64))
            return 0
        lax.fori_loop(0, 4, chunk, 0)
        send_tile(l, 1, 3, y_dev, pl.ds(pl.multiple_of((12 + y) * 64, 64), 64))
        for m in (1, 2):
            @pl.when(x >= m)
            def _():
                wait_tiles(drs, l, 0, m, 3)
                send_tile(l, 1, m, x_dev, pl.ds(pl.multiple_of(x * 256, 256), 256))

    def wait_d(l):
        wait_tiles(drs, l, 1, 0, 12)
        wait_tiles(drs, l, 1, 3, 3)
        for m in (1, 2):
            @pl.when(x >= m)
            def _():
                wait_tiles(drs, l, 1, m, 4 * (3 - m))

            @pl.when(x < m)
            def _():
                wait_tiles(drs, l, 1, m, 4 * (4 - m))

    def place(l, b):
        rows = lax.broadcasted_iota(jnp.int32, (128, 128), 0)
        return jnp.where(rows == rmap[l, b], 1.0, 0.0).astype(BF16)

    wait_all(y0.at[pl.ds(0, 15)], rsem.at[S_Y0])
    for i in range(8):
        yt[0, :, i * 128:i * 128 + 128] = y0[2 * i:2 * i + 2].reshape(128, 128).astype(F32).T.astype(BF16)

    def forward(l, _):
        pltpu.make_async_copy(panel_hbm.at[l], panel.at[l], psem.at[l]).wait()

        def pair(n, _):
            u = nt(yt[l], panel[l, n * 256:n * 256 + 256, :]).astype(BF16)
            a = nt(u[:, :128], place(l, 2 * n)).reshape(N, 8, 128)
            b = nt(u[:, 128:], place(l, 2 * n + 1)).reshape(N, 8, 128)
            s1[l, :, n * 16:n * 16 + 16, :] = jnp.concatenate([a, b], axis=1).astype(BF16)
            return 0
        for n in range(4):
            pair(n, 0)
        early, late = pl.ds(0, 64), pl.ds(64, 48)
        spread(plane_dev, lambda to: s1.at[l, to[1], early, :], r1.at[l, c, early, :], S_F1 + l)
        for n in range(4, 7):
            pair(n, 0)
        spread(plane_dev, lambda to: s1.at[l, to[1], late, :], r1.at[l, c, late, :], S_G1 + l)
        r1[l, c, 0:112, :] = s1[l, c]
        build_e(l)
        start_d(l + 1)
        wait_all(r1.at[l, pl.ds(0, 15), early, :], rsem.at[S_F1 + l])
        wait_all(r1.at[l, pl.ds(0, 15), late, :], rsem.at[S_G1 + l])

        forward_d(l + 1)

        def owners(parity, q):
            rows = pl.ds(pl.multiple_of(parity * 512 + q * 256, 256), 256)
            return nn(emat[rows, :], r1[l].reshape(2048, 128)).reshape(4, 64, 128)
        for q in range(2):
            s2[l, 8 + q * 4:12 + q * 4] = owners(1 - k, q).astype(BF16)
        to_sibling = remote(s2.at[l, pl.ds(8, 8)], rsib.at[l], sibling, S_FS + l)
        to_sibling.start()
        for q in range(2):
            half[q * 4:q * 4 + 4] = owners(k, q)
        to_sibling.wait_recv()
        s2[l, 0:8] = (half[...] + rsib[l].astype(F32)).astype(BF16)
        r2[l, z] = s2[l, z]
        spread(z_dev, lambda to: s2.at[l, to[0] // 2], r2.at[l, z], S_F2 + l, 8)
        wait_all(r2.at[l, pl.ds(0, 7)], rsem.at[S_F2 + l])
        carried = jnp.sum(r2[l].astype(F32), axis=0)
        s3[l] = (rhsc[l + 1] - carried).astype(BF16)
        r3[l, c] = s3[l]
        spread(plane_dev, lambda to: s3.at[l], r3.at[l, c], S_F3 + l)
        wait_all(r3.at[l, pl.ds(0, 15)], rsem.at[S_F3 + l])
        got = r3[l].astype(F32).reshape(N, 8, 8, 128)
        for tb in range(8):
            ct[:, tb * 128:tb * 128 + 128] = got[:, tb].reshape(128, 128).astype(BF16)
        wait_d(l + 1)
        for i in range(4):
            e = 256 * (i + 1)
            yt[l + 1, :, i * 256:e] = sum(
                nt(ct[:, m * 256:m * 256 + 256], dfull[l + 1, m, i * 256:e, :]) for m in range(i + 1)).astype(BF16)
        return 0

    lax.fori_loop(0, 3, forward, 0)

    def back_solve(l):
        for m in range(4):
            xf[:, m * 256:m * 256 + 256] = nn(wt[:, m * 256:], dfull[l, m, m * 256:, :])

    def my_rows(tile_value):
        tile[...] = tile_value.T
        return tile[pl.ds(pl.multiple_of(lax.rem(c, 2) * 64, 64), 64), :].astype(BF16)

    wt[...] = yt[3]
    back_solve(3)
    mine8 = pl.ds(pl.multiple_of(c * 8, 8), 8)
    for tb in range(0, 8, 2):
        sb1[2, tb * 8:tb * 8 + 16, :] = jnp.concatenate(
            [xf[mine8, tb * 128:tb * 128 + 128], xf[mine8, tb * 128 + 128:tb * 128 + 256]], axis=0).astype(BF16)
    my_tile = c // 2

    def backward_to_partials(l):
        rb1[l, z] = sb1[l]
        spread(z_dev, lambda to: sb1.at[l], rb1.at[l, z], S_B1 + l, 8)
        build_et(l, ematt=emat_t)
        if not isinstance(l, int):
            @pl.when(l == 2)
            def _():
                start_d(0)

            @pl.when(l == 1)
            def _():
                forward_d(0)
        wait_all(rb1.at[l, pl.ds(0, 7)], rsem.at[S_B1 + l])
        to_sibling = remote(rb1.at[l], rbs.at[l], sibling, S_BS + l)
        to_sibling.start()
        mine = pl.ds(pl.multiple_of(k * 512, 512), 512)
        others = pl.ds(pl.multiple_of((1 - k) * 512, 512), 512)
        for n in range(4):
            gacc[n * 512:n * 512 + 512, :] = nn(emat_t[n * 512:n * 512 + 512, mine], rb1[l].reshape(512, 128))
        to_sibling.wait_recv()

        def holders(n, _):
            pair = lax.rem(c // 2 + n, 8)
            rows = pl.ds(pl.multiple_of(pair * 256, 256), 256)
            value = gacc[rows, :] + nn(emat_t[rows, others], rbs[l].reshape(512, 128))
            s4[l, pl.ds(pair * 2, 2)] = value.astype(BF16).reshape(2, 128, 128)
            for q in range(2):
                to = pair * 2 + q

                @pl.when(to != c)
                def _():
                    remote(s4.at[l, to, pl.ds(0, 112), :], r4.at[l, c], (p, to), S_B2 + l).start()
            return 0
        lax.fori_loop(0, 8, holders, 0)
        r4[l, c] = s4[l, c, 0:112, :]

    def backward_rest(l):
        wait_all(r4.at[l, pl.ds(0, 15)], rsem.at[S_B2 + l])

        def pair(n, _):
            got = r4[l, :, n * 16:n * 16 + 16, :].astype(F32)
            a = nn(got[:, :8].reshape(128, 128).astype(BF16), place(l, 2 * n))
            b = nn(got[:, 8:].reshape(128, 128).astype(BF16), place(l, 2 * n + 1))
            gt[:, n * 256:n * 256 + 256] = jnp.concatenate([a, b], axis=1).astype(BF16)
            return 0
        for n in range(7):
            pair(n, 0)

        def columns(n, _):
            cols = slice(n * 256, n * 256 + 256)
            t = nn(gt[...], panel[l, :, cols])
            wt[:, cols] = (yt[l, :, cols].astype(F32) * (1.0 / 16) - t).astype(BF16)
            return 0
        for n in range(4):
            columns(n, 0)
        back_solve(l)

    emat_t = tt

    def backward(m, _):
        l = 2 - m
        backward_to_partials(l)

        backward_rest(l)
        for tb in range(0, 8, 2):
            a = xf[:, tb * 128:tb * 128 + 128].reshape(N, 8, 128)
            b = xf[:, tb * 128 + 128:tb * 128 + 256].reshape(N, 8, 128)
            s5[l, :, tb * 8:tb * 8 + 16, :] = jnp.concatenate([a, b], axis=1).astype(BF16)
        r5[l, c] = s5[l, c]
        spread(plane_dev, lambda to: s5.at[l, to[1]], r5.at[l, c], S_B3 + l)
        wait_all(r5.at[l, pl.ds(0, 15)], rsem.at[S_B3 + l])
        total = jnp.sum(r5[l].astype(F32), axis=0).astype(BF16)
        sb1[l - 1] = total
        so[l] = total.astype(F32).reshape(8, 8, 128)
        ro[l, c] = so[l, my_tile]
        spread(plane_dev, lambda to: so.at[l, to[1] // 2], ro.at[l, c], S_OUT + l)
        return 0

    out[3] = my_rows(xf[:, pl.ds(pl.multiple_of(my_tile * 128, 128), 128)])
    lax.fori_loop(0, 2, backward, 0)
    backward_to_partials(0)
    for l in (2, 1):
        wait_all(ro.at[l, pl.ds(0, 15)], rsem.at[S_OUT + l])
        out[l] = my_rows(ro[l].reshape(128, 128))
    wait_d(0)
    backward_rest(0)
    for i in range(8):
        s7[2 * i:2 * i + 2] = xf[:, i * 128:i * 128 + 128].T.astype(BF16).reshape(2, 64, 128)
    r7[c] = s7[c]
    spread(plane_dev, lambda to: s7.at[to[1]], r7.at[c], S_X0)
    wait_all(r7.at[pl.ds(0, 15)], rsem.at[S_X0])
    out[0] = jnp.sum(r7[...].astype(F32), axis=0).astype(BF16)

    wait_all(c0.at[pl.ds(0, 15)], ssem.at[S_C0])
    wait_all(y0.at[pl.ds(0, 15)], ssem.at[S_Y0])
    wait_all(vall.at[pl.ds(0, 15)], ssem.at[S_V])
    wait_all(rr.at[pl.ds(0, 15)], ssem.at[S_R])
    wait_all(r7.at[pl.ds(0, 15)], ssem.at[S_X0])
    for l in range(3):
        wait_all(s1.at[l, pl.ds(0, 15), pl.ds(0, 64), :], ssem.at[S_F1 + l])
        wait_all(s1.at[l, pl.ds(0, 15), pl.ds(64, 48), :], ssem.at[S_G1 + l])
        wait_all(rsib.at[l], ssem.at[S_FS + l])
        wait_all(rbs.at[l], ssem.at[S_BS + l])
        wait_all(r2.at[l, pl.ds(0, 7)], ssem.at[S_F2 + l])
        wait_all(r3.at[l, pl.ds(0, 15)], ssem.at[S_F3 + l])
        wait_all(rb1.at[l, pl.ds(0, 7)], ssem.at[S_B1 + l])
        wait_all(r4.at[l, pl.ds(0, 15)], ssem.at[S_B2 + l])
        if l > 0:
            wait_all(s5.at[l, pl.ds(0, 15)], ssem.at[S_B3 + l])
            wait_all(ro.at[l, pl.ds(0, 15)], ssem.at[S_OUT + l])
    for l in range(4):
        wait_tiles(dss, l, 1, 0, 12)
        wait_tiles(dss, l, 1, 3, 3)
        for m in range(4):
            @pl.when(x >= m)
            def _():
                wait_tiles(dss, l, 0, m, 3)
                if m in (1, 2):
                    wait_tiles(dss, l, 1, m, 12)


def shards(rhs, diag_inv, panel, owner, target_block, row_map):
    vm = pl.BlockSpec(memory_space=pltpu.VMEM)
    b = lambda *s: pltpu.VMEM(s, BF16)
    f = lambda *s: pltpu.VMEM(s, F32)
    scratch = [
        b(3, 1792, 1024),
        b(4, 4, 1024, 256),
        b(1024, 2048),
        b(16, 64, 128), b(16, 64, 128),
        b(16, 32, 128), b(16, 32, 128), f(4, 64, 128),
        pltpu.VMEM((16, 8, 128), jnp.int32),
        b(4, 128, 1024), b(128, 1024),
        b(3, 16, 112, 128), b(3, 16, 128, 128),
        b(3, 16, 64, 128), b(3, 8, 64, 128),
        b(3, 64, 128), b(3, 16, 64, 128),
        b(3, 64, 128), b(3, 8, 64, 128),
        b(3, 16, 128, 128), b(3, 16, 112, 128),
        b(128, 1792), b(2048, 1024), b(128, 1024),
        b(3, 16, 64, 128), b(3, 16, 64, 128),
        f(3, 8, 8, 128), f(3, 16, 8, 128),
        b(16, 64, 128), b(16, 64, 128),
        f(128, 1024), f(128, 128), f(8, 128), f(8, 64, 128),
        b(3, 8, 64, 128), b(3, 8, 64, 128), f(2048, 128),
        pltpu.SemaphoreType.DMA((3,)), pltpu.SemaphoreType.DMA((NSEM,)), pltpu.SemaphoreType.DMA((NSEM,)),
        pltpu.SemaphoreType.DMA((4, 8)), pltpu.SemaphoreType.DMA((4, 8)),
    ]
    got = pl.pallas_call(
        kernel,
        out_shape=jax.ShapeDtypeStruct((4, 64, 128), BF16),
        in_specs=[vm, vm, pl.BlockSpec(memory_space=pl.ANY), vm, vm, vm],
        out_specs=vm,
        scratch_shapes=scratch,
        compiler_params=pltpu.CompilerParams(
            collective_id=0, has_side_effects=True, vmem_limit_bytes=58 << 20),
    )(rhs[:, 0], diag_inv[:, 0], panel[:, 0], owner.reshape(3, 1, 14), target_block, jnp.transpose(row_map, (0, 2, 1, 3)))
    return got[:, None]


def solution(mesh):
    return jax.shard_map(
        shards,
        mesh=mesh,
        in_specs=(
            P(None, "prow", "pcol", None),
            P(None, "prow", "pcol", None),
            P(None, "prow", "pcol", None),
            P(None, "prow", "pcol", None),
            P(None, "prow", "pcol"),
            P(None, "prow", "pcol", None),
        ),
        out_specs=P(None, "prow", "pcol", None),
        check_vma=False,
    )
```

time: 228 us -> 188 us (0.82)
  Pallas kernels: 222 us -> 186 us
    pallas_call x1, Pallas kernels: 222 us -> 186 us  [shards(): pl.pallas_call(kernel, out_shape=jax.ShapeDtypeStruct((4, 64, 128), BF16)...]
where the time goes in v2:
time: 188 us
  Pallas kernels  186 us (99%)
    pallas_call x1, Pallas kernels, shards(): pl.pallas_call(kernel, out_shape=jax.ShapeDtypeStruct((4, 64, 128), BF16)...  186 us

profile of v2, /device:TPU:1, one launch (start us, length us, event | category | flops | bytes accessed | tf_op | source)
XLA Modules:
  0.0 187.8 jit_solution(12981284336829651456)
XLA Ops:
  0.0 186.3 %shard_map.64 = bf16[4,64,128]{2,1,0:T(8,128)(2,1)} custom-call(bf16[4,64,128]{2,1,0:T(8,128)(2,1)} %bitcast.11, bf16[4,64,1024]{2,1,0:T(8,128)(2,1)} %bitcast.9, bf16[3,1792,1024]{2,1,0:T(8,128)(2,1)} %bitcast.8, s32[3,1,14]{2,1,0:T(1,128)} %bitcast.13, s32[3,1,14]{2,1,0:T(1,128)} %tblock.1, s32[3,14,1,128]{3,2,1,0:T(1,128)} %bitcast.12), custom_call_target="tpu_custom_call" | custom-call | tf_op jit(solution)/shard_map/pallas_call | solution.py:415
  186.4 1.5 copy.9

commit v3 on v2

--- a/solution.py
+++ b/solution.py
@@ -95,6 +95,19 @@
     spread(plane_dev, lambda to: c0.at[c], c0.at[c], S_C0)
     spread(plane_dev, lambda to: vall.at[c], vall.at[c], S_V)
     spread(plane_dev, lambda to: sr.at[to[1]], rr.at[c], S_R)
+
+    def place_rows(l):
+        pltpu.make_async_copy(panel_hbm.at[l], panel.at[l], psem.at[l]).wait()
+        rows = lax.broadcasted_iota(jnp.int32, (128, 128), 0)
+
+        def one(b, _):
+            block = pl.ds(pl.multiple_of(b * 128, 128), 128)
+            placed = jnp.where(rows == rmap[l, b], 1.0, 0.0).astype(BF16)
+            panel[l, block, :] = nn(placed, panel[l, block, :]).astype(BF16)
+            return 0
+        lax.fori_loop(0, 14, one, 0)
+
+    place_rows(0)
     wait_all(c0.at[pl.ds(0, 15)], rsem.at[S_C0])
     y0[c] = nn(dinv[0], c0[...].reshape(1024, 128)).astype(BF16)
     spread(plane_dev, lambda to: y0.at[c], y0.at[c], S_Y0)
@@ -186,21 +199,16 @@
             def _():
                 wait_tiles(drs, l, 1, m, 4 * (4 - m))
 
-    def place(l, b):
-        rows = lax.broadcasted_iota(jnp.int32, (128, 128), 0)
-        return jnp.where(rows == rmap[l, b], 1.0, 0.0).astype(BF16)
-
     wait_all(y0.at[pl.ds(0, 15)], rsem.at[S_Y0])
+    start_d(1)
     for i in range(8):
         yt[0, :, i * 128:i * 128 + 128] = y0[2 * i:2 * i + 2].reshape(128, 128).astype(F32).T.astype(BF16)
 
     def forward(l, _):
-        pltpu.make_async_copy(panel_hbm.at[l], panel.at[l], psem.at[l]).wait()
-
         def pair(n, _):
-            u = nt(yt[l], panel[l, n * 256:n * 256 + 256, :]).astype(BF16)
-            a = nt(u[:, :128], place(l, 2 * n)).reshape(N, 8, 128)
-            b = nt(u[:, 128:], place(l, 2 * n + 1)).reshape(N, 8, 128)
+            u = nt(yt[l], panel[l, n * 256:n * 256 + 256, :])
+            a = u[:, :128].reshape(N, 8, 128)
+            b = u[:, 128:].reshape(N, 8, 128)
             s1[l, :, n * 16:n * 16 + 16, :] = jnp.concatenate([a, b], axis=1).astype(BF16)
             return 0
         for n in range(4):
@@ -212,11 +220,9 @@
         spread(plane_dev, lambda to: s1.at[l, to[1], late, :], r1.at[l, c, late, :], S_G1 + l)
         r1[l, c, 0:112, :] = s1[l, c]
         build_e(l)
-        start_d(l + 1)
         wait_all(r1.at[l, pl.ds(0, 15), early, :], rsem.at[S_F1 + l])
         wait_all(r1.at[l, pl.ds(0, 15), late, :], rsem.at[S_G1 + l])
 
-        forward_d(l + 1)
 
         def owners(parity, q):
             rows = pl.ds(pl.multiple_of(parity * 512 + q * 256, 256), 256)
@@ -225,18 +231,24 @@
             s2[l, 8 + q * 4:12 + q * 4] = owners(1 - k, q).astype(BF16)
         to_sibling = remote(s2.at[l, pl.ds(8, 8)], rsib.at[l], sibling, S_FS + l)
         to_sibling.start()
+        forward_d(l + 1)
         for q in range(2):
             half[q * 4:q * 4 + 4] = owners(k, q)
         to_sibling.wait_recv()
         s2[l, 0:8] = (half[...] + rsib[l].astype(F32)).astype(BF16)
         r2[l, z] = s2[l, z]
         spread(z_dev, lambda to: s2.at[l, to[0] // 2], r2.at[l, z], S_F2 + l, 8)
+
+        @pl.when(l < 2)
+        def _():
+            place_rows(l + 1)
         wait_all(r2.at[l, pl.ds(0, 7)], rsem.at[S_F2 + l])
         carried = jnp.sum(r2[l].astype(F32), axis=0)
         s3[l] = (rhsc[l + 1] - carried).astype(BF16)
         r3[l, c] = s3[l]
         spread(plane_dev, lambda to: s3.at[l], r3.at[l, c], S_F3 + l)
         wait_all(r3.at[l, pl.ds(0, 15)], rsem.at[S_F3 + l])
+        start_d(lax.rem(l + 2, 4))
         got = r3[l].astype(F32).reshape(N, 8, 8, 128)
         for tb in range(8):
             ct[:, tb * 128:tb * 128 + 128] = got[:, tb].reshape(128, 128).astype(BF16)
@@ -270,10 +282,6 @@
         spread(z_dev, lambda to: sb1.at[l], rb1.at[l, z], S_B1 + l, 8)
         build_et(l, ematt=emat_t)
         if not isinstance(l, int):
-            @pl.when(l == 2)
-            def _():
-                start_d(0)
-
             @pl.when(l == 1)
             def _():
                 forward_d(0)
@@ -306,8 +314,8 @@
 
         def pair(n, _):
             got = r4[l, :, n * 16:n * 16 + 16, :].astype(F32)
-            a = nn(got[:, :8].reshape(128, 128).astype(BF16), place(l, 2 * n))
-            b = nn(got[:, 8:].reshape(128, 128).astype(BF16), place(l, 2 * n + 1))
+            a = got[:, :8].reshape(128, 128)
+            b = got[:, 8:].reshape(128, 128)
             gt[:, n * 256:n * 256 + 256] = jnp.concatenate([a, b], axis=1).astype(BF16)
             return 0
         for n in range(7):

time: 188 us -> 183 us (0.973)
  Pallas kernels: 186 us -> 181 us
    pallas_call x1, Pallas kernels: 186 us -> 181 us  [shards(): pl.pallas_call(kernel, out_shape=jax.ShapeDtypeStruct((4, 64, 128), BF16)...]
where the time goes in v3:
time: 183 us
  Pallas kernels  181 us (99%)
    pallas_call x1, Pallas kernels, shards(): pl.pallas_call(kernel, out_shape=jax.ShapeDtypeStruct((4, 64, 128), BF16)...  181 us

profile of v3, /device:TPU:1, one launch (start us, length us, event | category | flops | bytes accessed | tf_op | source)
XLA Modules:
  0.0 182.9 jit_solution(2739142888758738859)
XLA Ops:
  0.0 181.4 %shard_map.64 = bf16[4,64,128]{2,1,0:T(8,128)(2,1)} custom-call(bf16[4,64,128]{2,1,0:T(8,128)(2,1)} %bitcast.11, bf16[4,64,1024]{2,1,0:T(8,128)(2,1)} %bitcast.9, bf16[3,1792,1024]{2,1,0:T(8,128)(2,1)} %bitcast.8, s32[3,1,14]{2,1,0:T(1,128)} %bitcast.13, s32[3,1,14]{2,1,0:T(1,128)} %tblock.1, s32[3,14,1,128]{3,2,1,0:T(1,128)} %bitcast.12), custom_call_target="tpu_custom_call" | custom-call | tf_op jit(solution)/shard_map/pallas_call | solution.py:423
  181.4 1.5 copy.9
